TPU v7x, 32 devices: a whole 2x2x4 slice. The times are simulated.
32 devices in a mesh: grp: 2 (over y), row: 8 (over z, x), sub: 2 (over core).
Axes of the slice: x: 2, y: 2, z: 4, core: 2. Of those that a mesh axis runs over, the one named last changes fastest.
Arguments:
- pair_rep: bfloat16 [64, 32, 128], P(('grp', 'row'), 'sub'), parts along dimension 0, may hold values from -6 to 6
- norm_gain: float32 [128], replicated, may hold values from 0.1 to 1.9
- norm_bias: float32 [128], replicated, may hold values from -3 to 3
- w_a_proj: bfloat16 [128, 128], replicated, may hold values from -0.5 to 0.5
- w_a_gate: bfloat16 [128, 128], replicated, may hold values from -0.5 to 0.5
- w_b_proj: bfloat16 [128, 128], replicated, may hold values from -0.5 to 0.5
- w_b_gate: bfloat16 [128, 128], replicated, may hold values from -0.5 to 0.5
- w_gate: bfloat16 [128, 128], replicated, may hold values from -0.5 to 0.5
- out_gain: float32 [128], replicated, may hold values from 0.1 to 1.9
- out_bias: float32 [128], replicated, may hold values from -3 to 3
- w_out: bfloat16 [128, 128], replicated, may hold values from -0.5 to 0.5
Outputs:
- update: bfloat16 [64, 32, 128], P(('grp', 'row'), 'sub'), parts along dimension 0
There are 2 independent parts, one for each index of `grp`. A program takes and returns all parts, laid end to end along the dimension named above; an argument that names none is the same for every part. Nothing has to cross between parts.
All inputs are finite; a program needn't handle non-finite values.
Results may differ from a plain program's by a relative error of at most 0.012.
Values may be sent and summed in bfloat16 or wider, within the bound.
A program may use at most 64 MiB of HBM per device.

v0:
```python
import jax
import jax.numpy as jnp
from jax import lax
from jax.sharding import PartitionSpec as P

EPSILON = 1e-05


def layer_norm(values, gain, shift, axis):
    centred = values - jnp.mean(values, axis=axis, keepdims=True)
    variance = jnp.mean(centred * centred, axis=axis, keepdims=True)
    return centred * lax.rsqrt(variance + EPSILON) * gain + shift


def per_device(
    pair_rep,
    norm_gain,
    norm_bias,
    w_a_proj,
    w_a_gate,
    w_b_proj,
    w_b_gate,
    w_gate,
    out_gain,
    out_bias,
    w_out,
):
    hidden = w_a_proj.shape[1]
    w_inner = jnp.concatenate([w_a_proj, w_a_gate, w_b_proj, w_b_gate], axis=1)
    normed = layer_norm(pair_rep.astype(jnp.float32), norm_gain, norm_bias, -1).astype(jnp.bfloat16)
    inner = jnp.einsum("rkc,cm->mrk", normed, w_inner, preferred_element_type=jnp.float32)
    left_local = (jax.nn.sigmoid(inner[hidden : 2 * hidden]) * inner[:hidden]).astype(jnp.bfloat16)
    right_local = (
        jax.nn.sigmoid(inner[3 * hidden : 4 * hidden]) * inner[2 * hidden : 3 * hidden]
    ).astype(jnp.bfloat16)
    gating = jax.nn.sigmoid(
        jnp.einsum("rkc,cd->rkd", normed, w_gate, preferred_element_type=jnp.float32)
    ).astype(jnp.bfloat16)
    left_chan, right_chan = (
        lax.all_to_all(left_local, "row", split_axis=0, concat_axis=1, tiled=True),
        lax.all_to_all(right_local, "row", split_axis=0, concat_axis=1, tiled=True),
    )
    left_rows = lax.all_to_all(left_chan, "sub", split_axis=1, concat_axis=2, tiled=True)
    triangle = jnp.einsum(
        "hik,hjk->hij",
        left_rows,
        lax.all_gather(right_chan, "sub", axis=2, tiled=True),
        preferred_element_type=jnp.float32,
    ).astype(jnp.bfloat16)
    regrouped = lax.all_to_all(
        lax.all_to_all(triangle, "sub", split_axis=2, concat_axis=1, tiled=True),
        "row",
        split_axis=1,
        concat_axis=0,
        tiled=True,
    )
    hidden_normed = layer_norm(
        regrouped.astype(jnp.float32), out_gain[:, None, None], out_bias[:, None, None], 0
    ).astype(jnp.bfloat16)
    mixed = jnp.einsum("hrj,hc->rjc", hidden_normed, w_out, preferred_element_type=jnp.float32)
    return (gating.astype(jnp.float32) * mixed).astype(jnp.bfloat16)


def solution(mesh):
    in_specs = (P(("grp", "row"), "sub", None), P(), P(), P(), P(), P(), P(), P(), P(), P(), P())
    out_specs = P(("grp", "row"), "sub", None)
    return jax.shard_map(
        per_device, mesh=mesh, in_specs=in_specs, out_specs=out_specs, check_vma=False
    )
```

profile of v0, /device:TPU:0, one launch (start us, length us, event | category | flops | bytes accessed | tf_op | source)
XLA Modules:
  0.0 51.0 jit_solution(15292789113996940466)
XLA Ops:
  0.0 0.0 copy-start
  0.0 0.0 copy-start.1
  0.0 0.9 %convert_reduce_fusion = f32[4,16]{1,0:T(4,128)S(1)} fusion(bf16[4,16,128]{2,1,0:T(8,128)(2,1)} %param.11), kind=kLoop, calls=%fused_computation.23 | loop fusion | flops 16320 | bytes 16640 | tf_op jit(solution)/shard_map/reduce_sum | solution.py:10
  0.9 0.0 copy-done.1
  0.9 0.2 fusion.16
  1.1 0.6 %copy-done.3 = f32[128]{0:T(128)S(1)} copy-done((f32[128]{0:T(128)S(1)}, f32[128]{0:T(128)}, u32[]{:S(2)}) %copy-start.3) | copy-done | bytes 536
  1.7 0.0 copy-done.4
  1.7 1.0 %fusion.7 = f32[512,4,16]{0,2,1:T(8,128)S(1)} fusion(bf16[128,128]{1,0:T(8,128)(2,1)} %param.17, bf16[128,128]{1,0:T(8,128)(2,1)} %param.16, bf16[128,128]{1,0:T(8,128)(2,1)} %param.15, bf16[128,128]{1,0:T(8,128)(2,1)} %param.14, bf16[4,16,128]{2,1,0:T(8,128)(2,1)S(1)} %copy-done.1, f32[128]{0:T(128)S(1)} %copy-done.3, f32[128]{0:T(128)S(1)} %copy-done.4, ...), kind=kOutput, calls=%fused_computation.13 | convolution fusion | flops 8962048 | bytes 280064 | tf_op jit(solution)/shard_map/rkc,cm->mrk/dot_general | solution.py:31
  2.8 0.1 copy.28
  2.9 0.8 %reshape.40 = bf16[8,2,512]{2,1,0:T(2,128)(2,1)} reshape(bf16[128,4,16]{2,1,0:T(4,128)(2,1)S(1)} %copy.28) | data formatting | bytes 32768
  3.7 7.3 %all-to-all-start = ((bf16[8,2,512]{2,1,0:T(2,128)(2,1)}), bf16[8,2,512]{2,1,0:T(2,128)(2,1)S(1)}, u32[]{:S(2)}, u32[]{:S(2)}) async-start(bf16[8,2,512]{2,1,0:T(2,128)(2,1)} %reshape.40), calls=%async_computation | async-start | bytes 32768 | tf_op jit(solution)/shard_map/all_to_all | solution.py:40
  10.9 0.1 copy.32
  11.1 0.8 %reshape.44 = bf16[8,2,512]{2,1,0:T(2,128)(2,1)} reshape(bf16[128,4,16]{2,1,0:T(4,128)(2,1)S(1)} %copy.32) | data formatting | bytes 32768
  11.9 5.7 %all-to-all-done = bf16[8,2,512]{2,1,0:T(2,128)(2,1)S(1)} async-done(((bf16[8,2,512]{2,1,0:T(2,128)(2,1)}), bf16[8,2,512]{2,1,0:T(2,128)(2,1)S(1)}, u32[]{:S(2)}, u32[]{:S(2)}) %all-to-all-start) | async-done | bytes 16416 | tf_op jit(solution)/shard_map/all_to_all | solution.py:40
  17.5 0.1 reshape.41
  17.7 0.2 reshape.42
  17.9 3.7 %all_to_all.81 = bf16[2,2,2048]{2,1,0:T(2,128)(2,1)S(1)} all-to-all(bf16[2,2,2048]{2,1,0:T(2,128)(2,1)S(1)} %reshape.42), channel_id=1, replica_groups=mesh['grp'=2,'row'=8,'sub'=2] {'sub'}, dimensions={0} | all-to-all | bytes 32768 | tf_op jit(solution)/shard_map/all_to_all | solution.py:43
  21.6 3.3 %all-to-all-start.2 = ((bf16[8,2,512]{2,1,0:T(2,128)(2,1)}), bf16[8,2,512]{2,1,0:T(2,128)(2,1)S(1)}, u32[]{:S(2)}, u32[]{:S(2)}) async-start(bf16[8,2,512]{2,1,0:T(2,128)(2,1)} %reshape.44), calls=%async_computation.2 | async-start | bytes 32768 | tf_op jit(solution)/shard_map/all_to_all | solution.py:41
  24.9 0.1 reshape.43
  25.1 0.1 copy.44
  25.2 0.1 all_to_all.66
  25.3 6.1 %all-to-all-done.2 = bf16[8,2,512]{2,1,0:T(2,128)(2,1)S(1)} async-done(((bf16[8,2,512]{2,1,0:T(2,128)(2,1)}), bf16[8,2,512]{2,1,0:T(2,128)(2,1)S(1)}, u32[]{:S(2)}, u32[]{:S(2)}) %all-to-all-start.2) | async-done | bytes 16416 | tf_op jit(solution)/shard_map/all_to_all | solution.py:41
  31.4 0.1 reshape.45
  31.6 0.2 copy.34
  31.8 1.9 %all_gather.3 = bf16[16,32,32]{1,2,0:T(8,128)(2,1)S(1)} all-gather(bf16[16,32,16]{1,2,0:T(8,128)(2,1)S(1)} %copy.34), channel_id=1, replica_groups=mesh['grp'=2,'row'=8,'sub'=2] {'sub'}, dimensions={2}, use_global_device_ids=true | all-gather | bytes 49152 | tf_op jit(solution)/shard_map/all_gather | solution.py:47
  33.7 0.2 convolution_convert_fusion
  33.8 0.2 copy.35
  34.0 0.2 reshape.46
  34.2 3.7 %all_to_all.82 = bf16[2,2,2048]{2,1,0:T(2,128)(2,1)S(1)} all-to-all(bf16[2,2,2048]{2,1,0:T(2,128)(2,1)S(1)} %reshape.46), channel_id=1, replica_groups=mesh['grp'=2,'row'=8,'sub'=2] {'sub'}, dimensions={0} | all-to-all | bytes 32768 | tf_op jit(solution)/shard_map/all_to_all | solution.py:51
  37.9 0.1 reshape.47
  38.0 0.1 copy.45
  38.2 0.2 copy.41
  38.4 0.8 %reshape.48 = bf16[8,2,512]{2,1,0:T(2,128)(2,1)} reshape(bf16[32,16,16]{2,1,0:T(8,128)(2,1)S(1)} %bitcast.60) | data formatting | bytes 32768
  39.1 3.3 %all-to-all-start.4 = ((bf16[8,2,512]{2,1,0:T(2,128)(2,1)}), bf16[8,2,512]{2,1,0:T(2,128)(2,1)S(1)}, u32[]{:S(2)}, u32[]{:S(2)}) async-start(bf16[8,2,512]{2,1,0:T(2,128)(2,1)} %reshape.48), calls=%async_computation.4 | async-start | bytes 32768 | tf_op jit(solution)/shard_map/all_to_all | solution.py:50
  42.5 0.0 copy-done
  42.5 0.2 fusion.4
  42.7 6.3 %all-to-all-done.4 = bf16[8,2,512]{2,1,0:T(2,128)(2,1)S(1)} async-done(((bf16[8,2,512]{2,1,0:T(2,128)(2,1)}), bf16[8,2,512]{2,1,0:T(2,128)(2,1)S(1)}, u32[]{:S(2)}, u32[]{:S(2)}) %all-to-all-start.4) | async-done | bytes 16416 | tf_op jit(solution)/shard_map/all_to_all | solution.py:50
  49.0 0.1 reshape.49
  49.2 0.1 multiply_reduce_fusion
  49.3 0.1 copy.38
  49.4 0.0 copy-start.2
  49.5 0.0 copy-start.5
  49.5 0.0 copy-start.6
  49.5 0.1 reshape.34
  49.6 0.6 %copy-done.2 = bf16[128,128]{1,0:T(8,128)(2,1)S(1)} copy-done((bf16[128,128]{1,0:T(8,128)(2,1)S(1)}, bf16[128,128]{1,0:T(8,128)(2,1)}, u32[]{:S(2)}) %copy-start.2) | copy-done | bytes 32792
  50.2 0.0 copy-done.5
  50.2 0.0 copy-done.6
  50.2 0.8 %fusion.5 = bf16[4,16,128]{2,1,0:T(8,128)(2,1)} fusion(f32[4,16,128]{2,1,0:T(8,128)S(1)} %fusion.4, bf16[128,128]{1,0:T(8,128)(2,1)S(1)} %copy-done.2, f32[128,4,16]{0,2,1:T(8,128)S(1)} %reshape.34, f32[128]{0:T(128)S(1)} %copy-done.5, f32[128]{0:T(128)S(1)} %copy-done.6, f32[4,16]{1,0:T(4,128)S(1)} %add_rsqrt_fusion, f32[4,16]{1,0:T(4,128)S(1)} %broadcast_multiply_fusion), kind=kOutput, calls=%fused_computation.8 | convolution fusion | flops 2154496 | bytes 116224 | tf_op jit(solution)/shard_map/hrj,hc->rjc/dot_general | solution.py:60
  (11 shorter events, 0.2 us)
Async XLA Ops:
  0.0 42.5 %copy-start = (bf16[128,128]{1,0:T(8,128)(2,1)S(1)}, bf16[128,128]{1,0:T(8,128)(2,1)}, u32[]{:S(2)}) copy-start(bf16[128,128]{1,0:T(8,128)(2,1)} %param.18) | copy-start | bytes 98308
  0.0 0.9 %copy-start.1 = (bf16[4,16,128]{2,1,0:T(8,128)(2,1)S(1)}, bf16[4,16,128]{2,1,0:T(8,128)(2,1)}, u32[]{:S(2)}) copy-start(bf16[4,16,128]{2,1,0:T(8,128)(2,1)} %param.11) | copy-start | bytes 49156
  1.0 0.7 %copy-start.3 = (f32[128]{0:T(128)S(1)}, f32[128]{0:T(128)}, u32[]{:S(2)}) copy-start(f32[128]{0:T(128)} %param.13) | copy-start | bytes 1540
  1.1 0.7 %copy-start.4 = (f32[128]{0:T(128)S(1)}, f32[128]{0:T(128)}, u32[]{:S(2)}) copy-start(f32[128]{0:T(128)} %param.12) | copy-start | bytes 1540
  3.7 13.8 %all-to-all-start = ((bf16[8,2,512]{2,1,0:T(2,128)(2,1)}), bf16[8,2,512]{2,1,0:T(2,128)(2,1)S(1)}, u32[]{:S(2)}, u32[]{:S(2)}) async-start(bf16[8,2,512]{2,1,0:T(2,128)(2,1)} %reshape.40), calls=%async_computation | async-start | bytes 32768 | tf_op jit(solution)/shard_map/all_to_all | solution.py:40
  21.6 9.8 %all-to-all-start.2 = ((bf16[8,2,512]{2,1,0:T(2,128)(2,1)}), bf16[8,2,512]{2,1,0:T(2,128)(2,1)S(1)}, u32[]{:S(2)}, u32[]{:S(2)}) async-start(bf16[8,2,512]{2,1,0:T(2,128)(2,1)} %reshape.44), calls=%async_computation.2 | async-start | bytes 32768 | tf_op jit(solution)/shard_map/all_to_all | solution.py:41
  39.1 9.9 %all-to-all-start.4 = ((bf16[8,2,512]{2,1,0:T(2,128)(2,1)}), bf16[8,2,512]{2,1,0:T(2,128)(2,1)S(1)}, u32[]{:S(2)}, u32[]{:S(2)}) async-start(bf16[8,2,512]{2,1,0:T(2,128)(2,1)} %reshape.48), calls=%async_computation.4 | async-start | bytes 32768 | tf_op jit(solution)/shard_map/all_to_all | solution.py:50
  49.4 0.8 %copy-start.2 = (bf16[128,128]{1,0:T(8,128)(2,1)S(1)}, bf16[128,128]{1,0:T(8,128)(2,1)}, u32[]{:S(2)}) copy-start(bf16[128,128]{1,0:T(8,128)(2,1)} %param.21) | copy-start | bytes 98308
  49.5 0.8 %copy-start.5 = (f32[128]{0:T(128)S(1)}, f32[128]{0:T(128)}, u32[]{:S(2)}) copy-start(f32[128]{0:T(128)} %param.20) | copy-start | bytes 1540
  49.5 0.7 %copy-start.6 = (f32[128]{0:T(128)S(1)}, f32[128]{0:T(128)}, u32[]{:S(2)}) copy-start(f32[128]{0:T(128)} %param.19) | copy-start | bytes 1540
where the time goes:
time: 51.6 us; the launch traced here: 51 us
  waiting for transfers between devices  18.1 us (35%)
  starting transfers between devices  13.9 us (27%)
  blocking collectives  9.33 us (18%)
  local copies, waits for them, and re-layouts  6.09 us (12%)
  matrix products  2.19 us (4%)
  other arithmetic  1.21 us (2%)
    all_to_all x1, starting transfers between devices, per_device(): lax.all_to_all(left_local, 'row', split_axis=0, concat_axis=1, tiled=True)  7.25 us
    all_to_all x1, waiting for transfers between devices, per_device(): lax.all_to_all(lax.all_to_all(triangle, 'sub', split_axis=2, concat_axis=...  6.28 us
    all_to_all x1, waiting for transfers between devices, per_device(): lax.all_to_all(right_local, 'row', split_axis=0, concat_axis=1, tiled=True)  6.1 us
    all_to_all x1, waiting for transfers between devices, per_device(): lax.all_to_all(left_local, 'row', split_axis=0, concat_axis=1, tiled=True)  5.67 us
    unnamed x24, local copies, waits for them, and re-layouts  4.59 us
    all_to_all x1, blocking collectives, per_device(): lax.all_to_all(triangle, 'sub', split_axis=2, concat_axis=1, tiled=True)  3.72 us
    all_to_all x1, blocking collectives, per_device(): lax.all_to_all(left_chan, 'sub', split_axis=1, concat_axis=2, tiled=True)  3.72 us
    all_to_all x1, starting transfers between devices, per_device(): lax.all_to_all(lax.all_to_all(triangle, 'sub', split_axis=2, concat_axis=...  3.34 us
  transfers between devices with their start and end apart: 3, of which 3 were waited for; matrix products, arithmetic and copies ran while one was open for 3% of the time, Pallas kernels for 0%

commit v1 on v0

--- a/solution.py
+++ b/solution.py
@@ -1,6 +1,10 @@
+import functools
+
 import jax
 import jax.numpy as jnp
 from jax import lax
+from jax.experimental import pallas as pl
+from jax.experimental.pallas import tpu as pltpu
 from jax.sharding import PartitionSpec as P
 
 EPSILON = 1e-05
@@ -61,9 +65,263 @@
     return (gating.astype(jnp.float32) * mixed).astype(jnp.bfloat16)
 
 
+def activations(normed, weights, hidden):
+    inner = jnp.dot(normed, weights, preferred_element_type=jnp.float32)
+    return (jax.nn.sigmoid(inner[:, hidden:]) * inner[:, :hidden]).astype(jnp.bfloat16)
+
+
+def kernel(
+    n_row,
+    pair_hbm,
+    ngain_hbm,
+    nbias_hbm,
+    wap_hbm,
+    wag_hbm,
+    wbp_hbm,
+    wbg_hbm,
+    wg_hbm,
+    ogain_hbm,
+    obias_hbm,
+    wo_hbm,
+    out_ref,
+    raw,
+    vec_v,
+    w_v,
+    wo_v,
+    norm_v,
+    tri_v,
+    result,
+    in_sem,
+    send_sem,
+    recv_sem,
+    result_sem,
+):
+    _, _, rows, cols, chan = raw.shape
+    hidden = tri_v.shape[-1]
+    half = n_row // 2
+    row = lax.axis_index("row")
+    sub = lax.axis_index("sub")
+    part = row // half
+    place = lax.rem(row, half)
+    mirror = lax.rem(row + half, n_row)
+    near = sub == part
+    far = jnp.logical_not(near)
+
+    def remote(src, dst, send, recv, target_row, target_sub):
+        return pltpu.make_async_remote_copy(
+            src_ref=src,
+            dst_ref=dst,
+            send_sem=send,
+            recv_sem=recv,
+            device_id={"row": target_row, "sub": target_sub},
+            device_id_type=pl.DeviceIdType.MESH,
+        )
+
+    loads = [
+        pltpu.make_async_copy(ngain_hbm, vec_v.at[0], in_sem.at[0]),
+        pltpu.make_async_copy(nbias_hbm, vec_v.at[1], in_sem.at[1]),
+        pltpu.make_async_copy(wbp_hbm, w_v.at[:, 0:hidden], in_sem.at[2]),
+        pltpu.make_async_copy(wbg_hbm, w_v.at[:, hidden : 2 * hidden], in_sem.at[3]),
+        pltpu.make_async_copy(wap_hbm, w_v.at[:, 2 * hidden : 3 * hidden], in_sem.at[4]),
+        pltpu.make_async_copy(wag_hbm, w_v.at[:, 3 * hidden : 4 * hidden], in_sem.at[5]),
+        pltpu.make_async_copy(wg_hbm, w_v.at[:, 4 * hidden : 4 * hidden + chan], in_sem.at[6]),
+        pltpu.make_async_copy(ogain_hbm, vec_v.at[2], in_sem.at[7]),
+        pltpu.make_async_copy(obias_hbm, vec_v.at[3], in_sem.at[8]),
+        pltpu.make_async_copy(wo_hbm, wo_v, in_sem.at[9]),
+    ]
+    own_load = pltpu.make_async_copy(pair_hbm, raw.at[place, sub], recv_sem.at[place, sub])
+
+    barrier = pltpu.get_barrier_semaphore()
+
+    def greet(target_row, target_sub):
+        pl.semaphore_signal(
+            barrier,
+            inc=1,
+            device_id={"row": target_row, "sub": target_sub},
+            device_id_type=pl.DeviceIdType.MESH,
+        )
+
+    @pl.when(near)
+    def _():
+        greet(mirror, 0)
+        greet(mirror, 1)
+        for step in range(1, half):
+            for source_sub in range(2):
+                greet(part * half + lax.rem(place + step, half), source_sub)
+        greet(row, 1 - sub)
+        own_load.start()
+        for load in loads:
+            load.start()
+
+    @pl.when(far)
+    def _():
+        greet(mirror, sub)
+
+    pl.semaphore_wait(barrier, half + 1)
+
+    to_mirror = remote(
+        pair_hbm, raw.at[half, sub], send_sem.at[half], recv_sem.at[half, sub], mirror, 1 - part
+    )
+    to_near = [
+        remote(
+            pair_hbm,
+            raw.at[place, sub],
+            send_sem.at[step],
+            recv_sem.at[place, sub],
+            part * half + lax.rem(place + step, half),
+            part,
+        )
+        for step in range(half)
+    ]
+    for step in range(half - 1, 0, -1):
+        to_near[step].start()
+
+    @pl.when(far)
+    def _():
+        to_near[0].start()
+
+    to_mirror.start()
+    send_result = remote(
+        result, out_ref, send_sem.at[half + 1], result_sem, mirror, sub
+    )
+
+    @pl.when(near)
+    def _():
+        def arrive(unit):
+            for source_sub in range(2):
+                pltpu.make_async_copy(
+                    pair_hbm, raw.at[unit, source_sub], recv_sem.at[unit, source_sub]
+                ).wait()
+            pair = raw[unit].astype(jnp.float32).reshape(2 * rows * cols, chan)
+            return layer_norm(pair, vec_v[0], vec_v[1], -1).astype(jnp.bfloat16)
+
+        def spread(act):
+            return act.astype(jnp.float32).reshape(2, rows, cols, hidden)
+
+        w_right = slice(0, 2 * hidden)
+        w_left = slice(2 * hidden, 4 * hidden)
+        for load in loads:
+            load.wait()
+
+        normed = arrive(place)
+        norm_v[0] = normed.reshape(2, rows * cols, chan)
+        rights = [spread(activations(normed, w_v[:, w_right], hidden))]
+        lefts = [spread(activations(normed, w_v[:, w_left], hidden))]
+        normed = arrive(half)
+        norm_v[1] = normed.reshape(2, rows * cols, chan)
+        lefts.append(spread(activations(normed, w_v[:, w_left], hidden)))
+        gated = norm_v[:, sub].reshape(2 * rows * cols, chan)
+        gating = jax.nn.sigmoid(
+            jnp.dot(
+                gated, w_v[:, 4 * hidden : 4 * hidden + chan], preferred_element_type=jnp.float32
+            )
+        ).astype(jnp.bfloat16)
+
+        for step in range(half):
+            unit = lax.rem(place + step, half)
+            if step == 0:
+                block = rights[0]
+            else:
+                block = spread(activations(arrive(unit), w_v[:, w_right], hidden))
+            for which in range(2):
+                for i in range(rows):
+                    prod = lefts[which][:, i][:, None] * block
+                    prod = prod[0] + prod[1]
+                    prod = jnp.sum(prod.reshape(rows, cols // 8, 8, hidden), axis=1)
+                    tri_v[which, i, unit] = jnp.sum(prod, axis=1)
+
+        tri = jnp.concatenate(
+            [
+                tri_v[which, i, unit]
+                for which in range(2)
+                for i in range(rows)
+                for unit in range(half)
+            ],
+            axis=0,
+        )
+        tri = tri.astype(jnp.bfloat16).astype(jnp.float32)
+        hidden_normed = layer_norm(tri, vec_v[2], vec_v[3], -1).astype(jnp.bfloat16)
+        mixed = jnp.dot(hidden_normed, wo_v[...], preferred_element_type=jnp.float32)
+        out = (gating.astype(jnp.float32) * mixed).astype(jnp.bfloat16)
+        out = out.reshape(2, rows, cols, chan)
+        result[...] = out[1]
+        send_result.start()
+        out_ref[...] = out[0]
+        send_result.wait_send()
+
+    @pl.when(far)
+    def _():
+        send_result.wait_recv()
+        to_near[0].wait_send()
+
+    to_mirror.wait_send()
+    for step in range(1, half):
+        to_near[step].wait_send()
+
+
+def one_round(n_row, pair_rep, norm_gain, norm_bias, *rest):
+    w_a_proj, w_a_gate, w_b_proj, w_b_gate, w_gate, out_gain, out_bias, w_out = rest
+    rows, cols, chan = pair_rep.shape
+    hidden = w_a_proj.shape[1]
+    half = n_row // 2
+    hbm = pl.BlockSpec(memory_space=pltpu.HBM)
+    return pl.pallas_call(
+        functools.partial(kernel, n_row),
+        out_shape=pltpu.VMEM((rows, cols, chan), jnp.bfloat16),
+        in_specs=[hbm] * 11,
+        out_specs=pl.BlockSpec(memory_space=pltpu.VMEM),
+        scratch_shapes=[
+            pltpu.VMEM((half + 1, 2, rows, cols, chan), jnp.bfloat16),
+            pltpu.VMEM((4, 1, chan), jnp.float32),
+            pltpu.VMEM((chan, 4 * hidden + chan), jnp.bfloat16),
+            pltpu.VMEM((hidden, chan), jnp.bfloat16),
+            pltpu.VMEM((2, 2, rows * cols, chan), jnp.bfloat16),
+            pltpu.VMEM((2, rows, half, rows, hidden), jnp.float32),
+            pltpu.VMEM((rows, cols, chan), jnp.bfloat16),
+            pltpu.SemaphoreType.DMA((10,)),
+            pltpu.SemaphoreType.DMA((half + 2,)),
+            pltpu.SemaphoreType.DMA((half + 1, 2)),
+            pltpu.SemaphoreType.DMA,
+        ],
+        compiler_params=pltpu.CompilerParams(
+            collective_id=0, has_side_effects=True, vmem_limit_bytes=16 * 2**20
+        ),
+    )(
+        *(
+            pltpu.with_memory_space_constraint(operand, pltpu.HBM)
+            for operand in (
+                pair_rep,
+                norm_gain.reshape(1, chan),
+                norm_bias.reshape(1, chan),
+                w_a_proj,
+                w_a_gate,
+                w_b_proj,
+                w_b_gate,
+                w_gate,
+                out_gain.reshape(1, hidden),
+                out_bias.reshape(1, hidden),
+                w_out,
+            )
+        )
+    )
+
+
+def body(n_row, n_sub, *operands):
+    rows, cols, _ = operands[0].shape
+    hidden = operands[3].shape[1]
+    gathered = cols * cols * n_sub * hidden * 2
+    if n_sub == 2 and n_row % 2 == 0 and cols % 16 == 0 and gathered <= 4 * 2**20:
+        return one_round(n_row, *operands)
+    return per_device(*operands)
+
+
 def solution(mesh):
     in_specs = (P(("grp", "row"), "sub", None), P(), P(), P(), P(), P(), P(), P(), P(), P(), P())
     out_specs = P(("grp", "row"), "sub", None)
     return jax.shard_map(
-        per_device, mesh=mesh, in_specs=in_specs, out_specs=out_specs, check_vma=False
-    )
+        functools.partial(body, mesh.shape["row"], mesh.shape["sub"]),
+        mesh=mesh,
+        in_specs=in_specs,
+        out_specs=out_specs,
+        check_vma=False,
+    )

time: 51.6 us -> 12.3 us (0.24)
  waiting for transfers between devices: 18.1 us -> 0 us
  starting transfers between devices: 13.9 us -> 0 us
  Pallas kernels: 0 us -> 11.5 us
  blocking collectives: 9.33 us -> 0 us
  local copies, waits for them, and re-layouts: 6.09 us -> 0.61 us
  matrix products: 2.19 us -> 0 us
  other arithmetic: 1.21 us -> 0 us
    all_to_all x3 -> x0, waiting for transfers between devices: 18.1 us -> none  [the longest x1 6.28 us: per_device(): lax.all_to_all(lax.all_to_all(triangle, 'sub', split_axis=2, concat_axis=...]
    all_to_all x3 -> x0, starting transfers between devices: 13.9 us -> none  [the longest x1 7.25 us: per_device(): lax.all_to_all(left_local, 'row', split_axis=0, concat_axis=1, tiled=True)]
    pallas_call x0 -> x1, Pallas kernels: none -> 11.5 us  [one_round(): pl.pallas_call(functools.partial(kernel, n_row), out_shape=pltpu.VMEM((ro...]
    all_to_all x2 -> x0, blocking collectives: 7.44 us -> none  [the longest x1 3.72 us: per_device(): lax.all_to_all(triangle, 'sub', split_axis=2, concat_axis=1, tiled=True)]
    unnamed x24 -> x1, local copies, waits for them, and re-layouts: 4.59 us -> 0.61 us
    dot_general x4 -> x0, matrix products: 2.19 us -> none  [the longest x1 1.01 us: per_device(): jnp.einsum('rkc,cm->mrk', normed, w_inner, preferred_element_type=jnp.flo...]
    all_gather x1 -> x0, blocking collectives: 1.89 us -> none  [per_device(): lax.all_gather(right_chan, 'sub', axis=2, tiled=True)]
    reduce_sum x4 -> x0, other arithmetic: 1.14 us -> none  [the longest x2 0.92 us: layer_norm(): centred = values - jnp.mean(values, axis=axis, keepdims=True)]
  transfers between devices with their start and end apart: 3 -> 0, of which waited for: 3 -> 0; matrix products, arithmetic and copies ran while one was open for 3% -> 0% of each run, Pallas kernels for 0% -> 0%
where the time goes in v1:
time: 12.3 us; the launch traced here: 12.1 us
  Pallas kernels  11.5 us (93%)
  local copies, waits for them, and re-layouts  0.61 us (5%)
    pallas_call x1, Pallas kernels, one_round(): pl.pallas_call(functools.partial(kernel, n_row), out_shape=pltpu.VMEM((ro...  11.5 us
    unnamed x1, local copies, waits for them, and re-layouts  0.61 us

profile of v1, /device:TPU:0, one launch (start us, length us, event | category | flops | bytes accessed | tf_op | source)
XLA Modules:
  0.0 12.1 jit_solution(12087938864077299504)
XLA Ops:
  0.0 11.5 %shard_map.109 = bf16[4,16,128]{2,1,0:T(8,128)(2,1)S(1)} custom-call(bf16[4,16,128]{2,1,0:T(8,128)(2,1)} %pair_hbm.1, f32[1,128]{1,0:T(1,128)} %bitcast.4, f32[1,128]{1,0:T(1,128)} %bitcast.5, bf16[128,128]{1,0:T(8,128)(2,1)} %wap_hbm.1, bf16[128,128]{1,0:T(8,128)(2,1)} %wag_hbm.1, bf16[128,128]{1,0:T(8,128)(2,1)} %wbp_hbm.1, bf16[128,128]{1,0:T(8,128)(2,1)} %wbg_hbm.1, ...), custom_call_target="tpu_custom_call" | custom-call | tf_op jit(solution)/shard_map/pallas_call | solution.py:268
  11.5 0.6 %copy.13 = bf16[4,16,128]{2,1,0:T(8,128)(2,1)} copy(bf16[4,16,128]{2,1,0:T(8,128)(2,1)S(1)} %shard_map.109) | data formatting | bytes 32768
